TPU v7x, 32 devices: a whole 2x2x4 slice. The times are simulated.
32 devices in a mesh: groups: 2 (over y), replay: 4 (over z), module: 2 (over x), half: 2 (over core).
Axes of the slice: x: 2, y: 2, z: 4, core: 2. Of those that a mesh axis runs over, the one named last changes fastest.
Arguments:
- new_factors: bfloat16 [128, 2, 64, 128], P(('groups', 'replay', 'module')), parts along dimension 0, may hold values from -0.5 to 0.5
- new_counts: int32 [128], P(('groups', 'replay', 'module')), parts along dimension 0, may hold values from 32 to 64
- new_ids: int32 [128], P(('groups', 'module', 'half')), parts along dimension 0, may hold values from 0 to 3071
- replay_grads: bfloat16 [6144, 2, 4096], P(('groups', 'replay'), 'module', 'half'), parts along dimension 0, may hold values from -0.75 to 0.75
- replay_ids: int32 [6144], P(('groups', 'replay')), parts along dimension 0, may hold values from 0 to 3071
- slot_module: int32 [2], replicated, may hold values from 0 to 1, each once
- output_inverse: float32 [2, 64, 64], replicated, as said below
- input_inverse: float32 [2, 64, 64], replicated, as said below
Outputs:
- scores: float32 [128, 3072], P(('groups', 'module', 'half'), 'replay'), parts along dimension 0
There are 2 independent parts, one for each index of `groups`. A program takes and returns all parts, laid end to end along the dimension named above; an argument that names none is the same for every part. Nothing has to cross between parts.
Inputs may be any that keep to these rules, and one draw needn't show every extreme that they name: `new_counts`: each new example has at least half of its token slots live, the live ones first. `slot_module`: each module sits in exactly one slot. `output_inverse`: symmetric with a positive diagonal. `input_inverse`: symmetric with a positive diagonal.
All inputs are finite; a program needn't handle non-finite values.
Results may differ from a plain program's by a relative error of at most 0.0029.
Values may be sent and summed in bfloat16 or wider, within the bound.
No kernel may reach another device: no remote copies, remote signals or barrier semaphores. Data moves between devices by JAX's collectives and lax.ppermute only.
A program may use at most 64 MiB of HBM per device.

v0:
```python
import jax
import jax.numpy as jnp
from jax import lax
from jax.sharding import PartitionSpec as P


def body(
    new_factors,
    new_counts,
    new_ids,
    replay_grads,
    replay_ids,
    slot_module,
    output_inverse,
    input_inverse,
):
    module_count = output_inverse.shape[0]
    feature_count = output_inverse.shape[1]
    token_count = new_factors.shape[2]
    row_share = replay_grads.shape[2] // feature_count
    token_index = lax.iota(jnp.int32, token_count)
    token_live = token_index[None, :] < new_counts[:, None]
    live_factors = jnp.where(token_live[:, None, :, None], new_factors, jnp.zeros((), jnp.bfloat16))
    selector = slot_module[:, None] == lax.iota(jnp.int32, module_count)[None, :]
    slot_factors = jnp.einsum(
        "sm,emtc->estc",
        selector.astype(jnp.bfloat16),
        live_factors,
        preferred_element_type=jnp.float32,
    ).astype(jnp.bfloat16)
    left_inverse = jnp.einsum(
        "sm,mrc->src", selector.astype(jnp.float32), output_inverse, precision=lax.Precision.HIGHEST
    )
    right_inverse = jnp.einsum(
        "sm,mrc->src", selector.astype(jnp.float32), input_inverse, precision=lax.Precision.HIGHEST
    )
    first_row = lax.axis_index("half") * row_share
    left_rows = lax.dynamic_slice_in_dim(left_inverse, first_row, row_share, 1)
    activations = slot_factors[:, :, :, :feature_count]
    output_grads = slot_factors[:, :, :, feature_count:]
    gradients = jnp.einsum(
        "estr,estc->esrc", output_grads, activations, preferred_element_type=jnp.float32
    )
    preconditioned = jnp.einsum(
        "srk,eskc->esrc", left_rows, gradients, precision=lax.Precision.HIGHEST
    )
    preconditioned = jnp.einsum(
        "esrk,skc->esrc", preconditioned, right_inverse, precision=lax.Precision.HIGHEST
    )
    local_rows = preconditioned.astype(jnp.bfloat16).reshape(
        preconditioned.shape[0], module_count, row_share * feature_count
    )
    regrouped = lax.all_to_all(local_rows, "module", split_axis=1, concat_axis=0, tiled=True)
    new_block = regrouped.reshape(regrouped.shape[0], -1)
    replay_rows = replay_grads.reshape(replay_grads.shape[0], -1)
    partials = lax.dot_general(
        lax.all_gather(new_block, "replay", axis=0, tiled=True),
        replay_rows,
        (((1,), (1,)), ((), ())),
        preferred_element_type=jnp.float32,
    )
    summed_scores = lax.psum_scatter(partials, ("module", "half"), scatter_dimension=0, tiled=True)
    self_pairs = new_ids[:, None] == replay_ids[None, :]
    return jnp.where(self_pairs, jnp.zeros((), jnp.float32), summed_scores)


def solution(mesh):
    in_specs = (
        P(("groups", "replay", "module"), None, None, None),
        P(("groups", "replay", "module")),
        P(("groups", "module", "half")),
        P(("groups", "replay"), "module", "half"),
        P(("groups", "replay")),
        P(),
        P(),
        P(),
    )
    out_specs = P(("groups", "module", "half"), "replay")
    return jax.shard_map(body, mesh=mesh, in_specs=in_specs, out_specs=out_specs, check_vma=False)
```

profile of v0, /device:TPU:0, one launch (start us, length us, event | category | flops | bytes accessed | tf_op | source)
XLA Modules:
  0.0 69.7 jit_solution(8169205786504913018)
XLA Ops:
  6.5 0.0 copy-start
  6.5 0.0 reduce-scatter.2.cloned.1.call-start
  6.5 0.9 %iota_compare_fusion = pred[8,64]{1,0:T(8,128)(4,1)S(1)} fusion(s32[8]{0:T(128)} %param.9), kind=kLoop, calls=%fused_computation.20 | loop fusion | flops 512 | bytes 544 | tf_op jit(solution)/shard_map/lt | solution.py:22
  7.4 1.2 %broadcast_select_fusion = bf16[8,2,64,128]{3,2,1,0:T(8,128)(2,1)S(1)} fusion(bf16[8,2,64,128]{3,2,1,0:T(8,128)(2,1)} %param.8, pred[8,64]{1,0:T(8,128)(4,1)S(1)} %iota_compare_fusion), kind=kLoop, calls=%fused_computation.12 | loop fusion | flops 131072 | bytes 524800 | tf_op jit(solution)/shard_map/jit(_where)/select_n | solution.py:23
  8.6 1.1 %fusion.2 = bf16[8,2,64,128]{3,1,2,0:T(2,128)(2,1)S(1)} fusion(bf16[8,2,64,128]{3,2,1,0:T(8,128)(2,1)S(1)} %broadcast_select_fusion, s32[2]{0:T(128)} %param.13), kind=kOutput, calls=%fused_computation.3 | convolution fusion | flops 655364 | bytes 524296 | tf_op jit(solution)/shard_map/sm,emtc->estc/dot_general | solution.py:25
  9.7 1.2 %fusion.19 = (bf16[8,2,64,64]{3,1,2,0:T(2,128)(2,1)S(1)}, bf16[8,2,64,64]{3,1,2,0:T(2,128)(2,1)}) fusion(bf16[8,2,64,128]{3,1,2,0:T(2,128)(2,1)S(1)} %fusion.2), kind=kLoop, calls=%fused_computation.29 | loop fusion | bytes 524288 | tf_op jit(solution)/shard_map/slice | solution.py:40
  10.9 1.2 %fusion.10 = f32[2,64,64]{2,0,1:T(2,128)S(1)} fusion(f32[2,64,64]{2,1,0:T(8,128)} %param.14, s32[2]{0:T(128)} %param.13), kind=kOutput, calls=%fused_computation.15 | convolution fusion | flops 196612 | bytes 65544 | tf_op jit(solution)/shard_map/sm,mrc->src/dot_general | solution.py:31
  12.1 1.2 %convolution_bitcast_fusion.1 = f32[2,64,64,1]{2,0,1,3:T(2,128)S(1)} fusion(f32[2,64,64]{2,1,0:T(8,128)} %param.15, s32[2]{0:T(128)} %param.13), kind=kOutput, calls=%fused_computation.7 | convolution fusion | flops 196612 | bytes 65544 | tf_op jit(solution)/shard_map/sm,mrc->src/dot_general | solution.py:34
  13.3 2.0 %fusion.5 = f32[8,2,64,64]{3,2,1,0:T(8,128)} fusion(bf16[8,2,64,64]{3,1,2,0:T(2,128)(2,1)} %get-tuple-element.6, bf16[8,2,64,64]{3,1,2,0:T(2,128)(2,1)S(1)} %get-tuple-element.5), kind=kOutput, calls=%fused_computation.9 | convolution fusion | flops 8388608 | bytes 524288 | tf_op jit(solution)/shard_map/estr,estc->esrc/dot_general | solution.py:41
  15.3 0.0 copy-start.1
  15.3 0.0 copy-start.2
  15.3 1.5 %convolution_bitcast_fusion = f32[8,2,32,64]{3,2,0,1:T(8,128)S(1)} fusion(f32[8,2,64,64]{3,2,1,0:T(8,128)} %fusion.5, f32[2,32,64]{2,0,1:T(2,128)S(1)} %constant_dynamic-slice_fusion), kind=kOutput, calls=%fused_computation.4 | convolution fusion | flops 25165824 | bytes 409600 | tf_op jit(solution)/shard_map/srk,eskc->esrc/dot_general | solution.py:44
  16.8 0.4 fusion.3
  17.1 0.2 reshape.33
  17.3 8.1 %all_to_all.15 = bf16[8,2,2048]{2,0,1:T(8,128)(2,1)S(1)} all-to-all(bf16[8,2,2048]{2,0,1:T(8,128)(2,1)S(1)} %reshape.33), channel_id=1, replica_groups=mesh['groups'=2,'replay'=4,'module'=2,'half'=2] {'module'}, dimensions={1} | all-to-all | bytes 131072 | tf_op jit(solution)/shard_map/all_to_all | solution.py:53
  25.5 14.1 %all_gather.3 = bf16[64,2048]{1,0:T(8,128)(2,1)S(1)} all-gather(bf16[16,2048]{1,0:T(8,128)(2,1)S(1)} %bitcast.37), channel_id=1, replica_groups=mesh['groups'=2,'replay'=4,'module'=2,'half'=2] {'replay'}, dimensions={0}, use_global_device_ids=true | all-gather | bytes 327680 | tf_op jit(solution)/shard_map/all_gather | solution.py:57
  39.6 0.0 copy-done
  39.6 1.8 %fusion = f32[64,768]{1,0:T(8,128)} fusion(bf16[64,2048]{1,0:T(8,128)(2,1)S(1)} %all_gather.3, bf16[768,1,2048]{2,0,1:T(8,128)(2,1)S(1)} %copy-done), kind=kOutput, calls=%fused_computation | convolution fusion | flops 201326592 | bytes 3604480 | tf_op jit(solution)/shard_map/dot_general | solution.py:56
  41.3 0.0 reduce-scatter.2.cloned.1.call-update
  41.4 20.0 %reduce-scatter.2.cloned.1.call-done = f32[16,768]{1,0:T(8,128)} async-done(((f32[64,768]{1,0:T(8,128)}), f32[16,768]{1,0:T(8,128)}) %reduce-scatter.2.cloned.1.call-update) | async-done | bytes 49168 | tf_op jit(solution)/shard_map/reduce_scatter | solution.py:62
  61.4 0.0 copy-done.1
  61.4 0.0 copy-done.2
  61.4 1.5 %compare_select_fusion = f32[16,768]{1,0:T(8,128)} fusion(f32[16,768]{1,0:T(8,128)} %reduce-scatter.2.cloned.1.call-done, s32[768]{0:T(1024)S(1)} %copy-done.1, s32[16]{0:T(128)S(1)} %copy-done.2), kind=kLoop, calls=%fused_computation.18 | loop fusion | flops 24576 | bytes 101440 | tf_op jit(solution)/shard_map/jit(_where)/select_n | solution.py:64
  (1 shorter events, 0.0 us)
Async XLA Ops:
  6.5 33.1 %copy-start = (bf16[768,1,2048]{2,0,1:T(8,128)(2,1)S(1)}, bf16[768,1,2048]{2,0,1:T(8,128)(2,1)}, u32[]{:S(2)}) copy-start(bf16[768,1,2048]{2,0,1:T(8,128)(2,1)} %param.11) | copy-start | bytes 9437188
  6.5 54.9 %reduce-scatter.2.cloned.1.call-start = ((), (), s32[]{:S(2)}) async-start(), calls=%async_computation.2 | async-start | bytes 245760 | tf_op jit(solution)/shard_map/reduce_scatter | solution.py:62
  15.3 46.1 %copy-start.1 = (s32[768]{0:T(1024)S(1)}, s32[768]{0:T(1024)}, u32[]{:S(2)}) copy-start(s32[768]{0:T(1024)} %param.12) | copy-start | bytes 9220
  15.3 46.1 %copy-start.2 = (s32[16]{0:T(128)S(1)}, s32[16]{0:T(128)}, u32[]{:S(2)}) copy-start(s32[16]{0:T(128)} %param.10) | copy-start | bytes 196
Sparse Core Ops, SparseCore 0:
  41.5 19.8 reduce-scatter.1
where the time goes:
time: 70.1 us; the launch traced here: 69.7 us
  blocking collectives  22.3 us (32%)
  waiting for transfers between devices  20.1 us (29%)
  between operations  13.5 us (19%)
  matrix products  9.08 us (13%)
  other arithmetic  3.53 us (5%)
  local copies, waits for them, and re-layouts  1.37 us (2%)
    reduce_scatter x1, waiting for transfers between devices, body(): lax.psum_scatter(partials, ('module', 'half'), scatter_dimension=0, tiled...  20 us
    all_gather x1, blocking collectives, body(): lax.all_gather(new_block, 'replay', axis=0, tiled=True)  14.1 us
    all_to_all x1, blocking collectives, body(): lax.all_to_all(local_rows, 'module', split_axis=1, concat_axis=0, tiled=T...  8.13 us
    dot_general x1, matrix products, body(): jnp.einsum('estr,estc->esrc', output_grads, activations, preferred_elemen...  2.02 us
    dot_general x1, matrix products, body(): lax.dot_general(lax.all_gather(new_block, 'replay', axis=0, tiled=True),...  1.75 us
    select_n x1, other arithmetic, body(): return jnp.where(self_pairs, jnp.zeros((), jnp.float32), summed_scores)  1.49 us
    dot_general x1, matrix products, body(): jnp.einsum('srk,eskc->esrc', left_rows, gradients, precision=lax.Precisio...  1.47 us
  transfers between devices with their start and end apart: 1, of which 1 were waited for; matrix products, arithmetic and copies ran while one was open for 0% of the time, Pallas kernels for 0%

commit v1 on v0

--- a/solution.py
+++ b/solution.py
@@ -50,16 +50,55 @@
     local_rows = preconditioned.astype(jnp.bfloat16).reshape(
         preconditioned.shape[0], module_count, row_share * feature_count
     )
-    regrouped = lax.all_to_all(local_rows, "module", split_axis=1, concat_axis=0, tiled=True)
-    new_block = regrouped.reshape(regrouped.shape[0], -1)
+    replay_count = lax.axis_size("replay")
+    half_count = lax.axis_size("half")
+    replay_place = lax.axis_index("replay")
+    module_place = lax.axis_index("module")
+    half_place = lax.axis_index("half")
+    blocks = []
+    for module_step in range(module_count):
+        slot = lax.rem(module_place + module_step, module_count)
+        outgoing = lax.dynamic_index_in_dim(local_rows, slot, 1, keepdims=False)
+        for replay_step in range(replay_count):
+            if module_step == 0 and replay_step == 0:
+                blocks.append(outgoing)
+                continue
+            pairs = [
+                (
+                    z * module_count + x,
+                    (z + replay_step) % replay_count * module_count + (x + module_step) % module_count,
+                )
+                for z in range(replay_count)
+                for x in range(module_count)
+            ]
+            blocks.append(lax.ppermute(outgoing, ("replay", "module"), pairs))
+    new_block = jnp.stack(blocks)
     replay_rows = replay_grads.reshape(replay_grads.shape[0], -1)
-    partials = lax.dot_general(
-        lax.all_gather(new_block, "replay", axis=0, tiled=True),
-        replay_rows,
-        (((1,), (1,)), ((), ())),
-        preferred_element_type=jnp.float32,
-    )
-    summed_scores = lax.psum_scatter(partials, ("module", "half"), scatter_dimension=0, tiled=True)
+    partials = jnp.einsum("bef,jf->bej", new_block, replay_rows, preferred_element_type=jnp.float32)
+    source = lax.iota(jnp.int32, replay_count * module_count)
+    replay_step = lax.rem(replay_place - source // module_count + replay_count, replay_count)
+    module_step = lax.rem(module_place - source % module_count + module_count, module_count)
+    partials = jnp.take(partials, module_step * replay_count + replay_step, axis=0)
+    partials = partials.reshape(module_count * half_count, -1, partials.shape[-1])
+    total = 0.0
+    for step in range(module_count * half_count):
+        module_step, half_step = step // half_count, step % half_count
+        target = lax.rem(module_place + module_step, module_count) * half_count + lax.rem(
+            half_place + half_step, half_count
+        )
+        chunk = lax.dynamic_index_in_dim(partials, target, 0, keepdims=False)
+        if step > 0:
+            pairs = [
+                (
+                    x * half_count + c,
+                    (x + module_step) % module_count * half_count + (c + half_step) % half_count,
+                )
+                for x in range(module_count)
+                for c in range(half_count)
+            ]
+            chunk = lax.ppermute(chunk, ("module", "half"), pairs)
+        total = total + chunk
+    summed_scores = total
     self_pairs = new_ids[:, None] == replay_ids[None, :]
     return jnp.where(self_pairs, jnp.zeros((), jnp.float32), summed_scores)
 

time: 70.1 us -> 38.6 us (0.55)
  blocking collectives: 22.3 us -> 0 us
  waiting for transfers between devices: 20.1 us -> 2.92 us
  starting transfers between devices: 0.01 us -> 15.2 us
  between operations: 13.5 us -> 0.17 us
  local copies, waits for them, and re-layouts: 1.37 us -> 7 us
    reduce_scatter x1 -> x0, waiting for transfers between devices: 20 us -> none  [body(): lax.psum_scatter(partials, ('module', 'half'), scatter_dimension=0, tiled...]
    ppermute x0 -> x10, starting transfers between devices: none -> 15.2 us  [the longest x7 13.2 us: body(): blocks.append(lax.ppermute(outgoing, ('replay', 'module'), pairs))]
    all_gather x1 -> x0, blocking collectives: 14.1 us -> none  [body(): lax.all_gather(new_block, 'replay', axis=0, tiled=True)]
    all_to_all x1 -> x0, blocking collectives: 8.13 us -> none  [body(): lax.all_to_all(local_rows, 'module', split_axis=1, concat_axis=0, tiled=T...]
    unnamed x6 -> x13, local copies, waits for them, and re-layouts: 0.01 us -> 4.26 us
    ppermute x0 -> x10, waiting for transfers between devices: none -> 2.92 us  [the longest x3 2.9 us: body(): chunk = lax.ppermute(chunk, ('module', 'half'), pairs)]
  transfers between devices with their start and end apart: 1 -> 10, of which waited for: 1 -> 2; matrix products, arithmetic and copies ran while one was open for 0% -> 12% of each run, Pallas kernels for 0% -> 0%
where the time goes in v1:
time: 38.6 us; the launch traced here: 38.3 us
  starting transfers between devices  15.2 us (39%)
  matrix products  9.31 us (24%)
  local copies, waits for them, and re-layouts  7 us (18%)
  other arithmetic  3.7 us (10%)
  waiting for transfers between devices  2.92 us (8%)
    ppermute x7, starting transfers between devices, body(): blocks.append(lax.ppermute(outgoing, ('replay', 'module'), pairs))  13.2 us
    unnamed x13, local copies, waits for them, and re-layouts  4.26 us
    ppermute x3, waiting for transfers between devices, body(): chunk = lax.ppermute(chunk, ('module', 'half'), pairs)  2.9 us
    dot_general x1, matrix products, body(): jnp.einsum('bef,jf->bej', new_block, replay_rows, preferred_element_type=...  2.03 us
    dot_general x1, matrix products, body(): jnp.einsum('estr,estc->esrc', output_grads, activations, preferred_elemen...  2.01 us
    ppermute x3, starting transfers between devices, body(): chunk = lax.ppermute(chunk, ('module', 'half'), pairs)  1.92 us
    select_n x1, other arithmetic, body(): return jnp.where(self_pairs, jnp.zeros((), jnp.float32), summed_scores)  1.52 us
    dot_general x1, matrix products, body(): jnp.einsum('srk,eskc->esrc', left_rows, gradients, precision=lax.Precisio...  1.45 us
  transfers between devices with their start and end apart: 10, of which 2 were waited for; matrix products, arithmetic and copies ran while one was open for 12% of the time, Pallas kernels for 0%

profile of v1, /device:TPU:0, one launch (start us, length us, event | category | flops | bytes accessed | tf_op | source)
XLA Modules:
  0.0 38.3 jit_solution(9858922003359775817)
XLA Ops:
  0.0 0.9 %iota_compare_fusion = pred[8,64]{1,0:T(8,128)(4,1)S(1)} fusion(s32[8]{0:T(128)} %param.9), kind=kLoop, calls=%fused_computation.40 | loop fusion | flops 512 | bytes 544 | tf_op jit(solution)/shard_map/lt | solution.py:22
  0.9 1.2 %broadcast_select_fusion = bf16[8,2,64,128]{3,2,1,0:T(8,128)(2,1)S(1)} fusion(bf16[8,2,64,128]{3,2,1,0:T(8,128)(2,1)} %param.8, pred[8,64]{1,0:T(8,128)(4,1)S(1)} %iota_compare_fusion), kind=kLoop, calls=%fused_computation.13 | loop fusion | flops 131072 | bytes 524800 | tf_op jit(solution)/shard_map/jit(_where)/select_n | solution.py:23
  2.1 1.1 %fusion.2 = bf16[8,2,64,128]{3,1,2,0:T(2,128)(2,1)S(1)} fusion(bf16[8,2,64,128]{3,2,1,0:T(8,128)(2,1)S(1)} %broadcast_select_fusion, s32[2]{0:T(128)} %param.13), kind=kOutput, calls=%fused_computation.4 | convolution fusion | flops 655364 | bytes 524296 | tf_op jit(solution)/shard_map/sm,emtc->estc/dot_general | solution.py:25
  3.2 1.2 %fusion.43 = (bf16[8,2,64,64]{3,1,2,0:T(2,128)(2,1)S(1)}, bf16[8,2,64,64]{3,1,2,0:T(2,128)(2,1)}) fusion(bf16[8,2,64,128]{3,1,2,0:T(2,128)(2,1)S(1)} %fusion.2), kind=kLoop, calls=%fused_computation.88 | loop fusion | bytes 524288 | tf_op jit(solution)/shard_map/slice | solution.py:40
  4.4 1.2 %fusion.10 = f32[2,64,64]{2,0,1:T(2,128)S(1)} fusion(f32[2,64,64]{2,1,0:T(8,128)} %param.14, s32[2]{0:T(128)} %param.13), kind=kOutput, calls=%fused_computation.17 | convolution fusion | flops 196612 | bytes 65544 | tf_op jit(solution)/shard_map/sm,mrc->src/dot_general | solution.py:31
  5.6 1.2 %convolution_bitcast_fusion.1 = f32[2,64,64,1]{2,0,1,3:T(2,128)S(1)} fusion(f32[2,64,64]{2,1,0:T(8,128)} %param.15, s32[2]{0:T(128)} %param.13), kind=kOutput, calls=%fused_computation.8 | convolution fusion | flops 196612 | bytes 65544 | tf_op jit(solution)/shard_map/sm,mrc->src/dot_general | solution.py:34
  6.7 2.0 %fusion.5 = f32[8,2,64,64]{3,2,1,0:T(8,128)} fusion(bf16[8,2,64,64]{3,1,2,0:T(2,128)(2,1)} %get-tuple-element.6, bf16[8,2,64,64]{3,1,2,0:T(2,128)(2,1)S(1)} %get-tuple-element.5), kind=kOutput, calls=%fused_computation.10 | convolution fusion | flops 8388608 | bytes 524288 | tf_op jit(solution)/shard_map/estr,estc->esrc/dot_general | solution.py:41
  8.8 1.5 %convolution_bitcast_fusion = f32[8,2,32,64]{3,2,0,1:T(8,128)S(1)} fusion(f32[8,2,64,64]{3,2,1,0:T(8,128)} %fusion.5, f32[2,32,64]{2,0,1:T(2,128)S(1)} %constant_dynamic-slice_fusion), kind=kOutput, calls=%fused_computation.5 | convolution fusion | flops 25165824 | bytes 409600 | tf_op jit(solution)/shard_map/srk,eskc->esrc/dot_general | solution.py:44
  10.2 0.4 fusion.3
  10.6 0.2 reshape.156
  10.8 3.1 %collective-permute-start = (bf16[8,2048]{1,0:T(8,128)(2,1)S(1)}, bf16[8,2048]{1,0:T(8,128)(2,1)S(1)}, u32[]{:S(2)}, u32[]{:S(2)}) collective-permute-start(bf16[8,2048]{1,0:T(8,128)(2,1)S(1)} %get-tuple-element.11), channel_id=1, source_target_pairs={{0,4},{2,6},{4,8},{6,10},{8,12},{10,14},{12,0},{14,2},{1,5},{3,7},... | collective-permute-start | bytes 98312 | tf_op jit(solution)/shard_map/ppermute | solution.py:74
  13.9 2.6 %collective-permute-start.1 = (bf16[8,2048]{1,0:T(8,128)(2,1)S(1)}, bf16[8,2048]{1,0:T(8,128)(2,1)S(1)}, u32[]{:S(2)}, u32[]{:S(2)}) collective-permute-start(bf16[8,2048]{1,0:T(8,128)(2,1)S(1)} %get-tuple-element.11), channel_id=1, source_target_pairs={{0,8},{2,10},{4,12},{6,14},{8,0},{10,2},{12,4},{14,6},{1,9},{3,11}... | collective-permute-start | bytes 98312 | tf_op jit(solution)/shard_map/ppermute | solution.py:74
  16.5 1.3 %collective-permute-start.2 = (bf16[8,2048]{1,0:T(8,128)(2,1)S(1)}, bf16[8,2048]{1,0:T(8,128)(2,1)S(1)}, u32[]{:S(2)}, u32[]{:S(2)}) collective-permute-start(bf16[8,2048]{1,0:T(8,128)(2,1)S(1)} %get-tuple-element.11), channel_id=1, source_target_pairs={{0,12},{2,14},{4,0},{6,2},{8,4},{10,6},{12,8},{14,10},{1,13},{3,15... | collective-permute-start | bytes 98312 | tf_op jit(solution)/shard_map/ppermute | solution.py:74
  17.8 1.5 %collective-permute-start.3 = (bf16[8,2048]{1,0:T(8,128)(2,1)S(1)}, bf16[8,2048]{1,0:T(8,128)(2,1)S(1)}, u32[]{:S(2)}, u32[]{:S(2)}) collective-permute-start(bf16[8,2048]{1,0:T(8,128)(2,1)S(1)} %get-tuple-element.10), channel_id=1, source_target_pairs={{0,2},{2,0},{4,6},{6,4},{8,10},{10,8},{12,14},{14,12},{1,3},{3,1},... | collective-permute-start | bytes 98312 | tf_op jit(solution)/shard_map/ppermute | solution.py:74
  19.3 0.7 %collective-permute-start.4 = (bf16[8,2048]{1,0:T(8,128)(2,1)S(1)}, bf16[8,2048]{1,0:T(8,128)(2,1)S(1)}, u32[]{:S(2)}, u32[]{:S(2)}) collective-permute-start(bf16[8,2048]{1,0:T(8,128)(2,1)S(1)} %get-tuple-element.10), channel_id=1, source_target_pairs={{0,6},{2,4},{4,10},{6,8},{8,14},{10,12},{12,2},{14,0},{1,7},{3,5},... | collective-permute-start | bytes 98312 | tf_op jit(solution)/shard_map/ppermute | solution.py:74
  20.0 0.6 %bitcast_dynamic-update-slice_fusion.7 = bf16[8,8,2048]{2,1,0:T(8,128)(2,1)} fusion(bf16[8,2,2048]{2,0,1:T(8,128)(2,1)S(1)} %reshape.156, s32[]{:T(128)S(6)} %select_n.93), kind=kLoop, calls=%fused_computation.35 | loop fusion | bytes 65540
  20.8 1.3 %collective-permute-start.5 = (bf16[8,2048]{1,0:T(8,128)(2,1)S(1)}, bf16[8,2048]{1,0:T(8,128)(2,1)S(1)}, u32[]{:S(2)}, u32[]{:S(2)}) collective-permute-start(bf16[8,2048]{1,0:T(8,128)(2,1)S(1)} %get-tuple-element.10), channel_id=1, source_target_pairs={{0,10},{2,8},{4,14},{6,12},{8,2},{10,0},{12,6},{14,4},{1,11},{3,9}... | collective-permute-start | bytes 98312 | tf_op jit(solution)/shard_map/ppermute | solution.py:74
  22.1 0.6 %bitcast_dynamic-update-slice_fusion.6 = bf16[8,8,2048]{2,1,0:T(8,128)(2,1)} fusion(bf16[8,8,2048]{2,1,0:T(8,128)(2,1)} %bitcast_dynamic-update-slice_fusion.7, bf16[8,2048]{1,0:T(8,128)(2,1)S(1)} %collective-permute-done), kind=kLoop, calls=%fused_computation.34 | loop fusion | bytes 65536
  22.7 2.8 %collective-permute-start.6 = (bf16[8,2048]{1,0:T(8,128)(2,1)S(1)}, bf16[8,2048]{1,0:T(8,128)(2,1)S(1)}, u32[]{:S(2)}, u32[]{:S(2)}) collective-permute-start(bf16[8,2048]{1,0:T(8,128)(2,1)S(1)} %get-tuple-element.10), channel_id=1, source_target_pairs={{0,14},{2,12},{4,2},{6,0},{8,6},{10,4},{12,10},{14,8},{1,15},{3,13... | collective-permute-start | bytes 98312 | tf_op jit(solution)/shard_map/ppermute | solution.py:74
  25.5 0.6 %bitcast_dynamic-update-slice_fusion.5 = bf16[8,8,2048]{2,1,0:T(8,128)(2,1)} fusion(bf16[8,8,2048]{2,1,0:T(8,128)(2,1)} %bitcast_dynamic-update-slice_fusion.6, bf16[8,2048]{1,0:T(8,128)(2,1)S(1)} %collective-permute-done.1), kind=kLoop, calls=%fused_computation.33 | loop fusion | bytes 65536
  26.1 0.6 %bitcast_dynamic-update-slice_fusion.4 = bf16[8,8,2048]{2,1,0:T(8,128)(2,1)} fusion(bf16[8,8,2048]{2,1,0:T(8,128)(2,1)} %bitcast_dynamic-update-slice_fusion.5, bf16[8,2048]{1,0:T(8,128)(2,1)S(1)} %collective-permute-done.2), kind=kLoop, calls=%fused_computation.32 | loop fusion | bytes 65536
  26.8 0.6 %bitcast_dynamic-update-slice_fusion.3 = bf16[8,8,2048]{2,1,0:T(8,128)(2,1)} fusion(bf16[8,8,2048]{2,1,0:T(8,128)(2,1)} %bitcast_dynamic-update-slice_fusion.4, bf16[8,2048]{1,0:T(8,128)(2,1)S(1)} %collective-permute-done.3), kind=kLoop, calls=%fused_computation.31 | loop fusion | bytes 65536
  27.4 0.6 %bitcast_dynamic-update-slice_fusion.2 = bf16[8,8,2048]{2,1,0:T(8,128)(2,1)} fusion(bf16[8,8,2048]{2,1,0:T(8,128)(2,1)} %bitcast_dynamic-update-slice_fusion.3, bf16[8,2048]{1,0:T(8,128)(2,1)S(1)} %collective-permute-done.4), kind=kLoop, calls=%fused_computation.30 | loop fusion | bytes 65536
  28.0 0.6 %bitcast_dynamic-update-slice_fusion.1 = bf16[8,8,2048]{2,1,0:T(8,128)(2,1)} fusion(bf16[8,8,2048]{2,1,0:T(8,128)(2,1)} %bitcast_dynamic-update-slice_fusion.2, bf16[8,2048]{1,0:T(8,128)(2,1)S(1)} %collective-permute-done.5), kind=kLoop, calls=%fused_computation.29 | loop fusion | bytes 65536
  28.6 0.6 %bitcast_dynamic-update-slice_fusion = bf16[8,8,2048]{2,1,0:T(8,128)(2,1)} fusion(bf16[8,8,2048]{2,1,0:T(8,128)(2,1)} %bitcast_dynamic-update-slice_fusion.1, bf16[8,2048]{1,0:T(8,128)(2,1)S(1)} %collective-permute-done.6), kind=kLoop, calls=%fused_computation.28 | loop fusion | bytes 65536 | tf_op jit(solution)/shard_map/stack | solution.py:75
  29.2 2.0 %fusion = f32[8,8,768]{2,1,0:T(8,128)S(1)} fusion(bf16[8,8,2048]{2,1,0:T(8,128)(2,1)} %bitcast_dynamic-update-slice_fusion, bf16[768,1,2048]{2,0,1:T(8,128)(2,1)S(1)} %copy-done), kind=kOutput, calls=%fused_computation.1 | convolution fusion | flops 201326592 | bytes 3604480 | tf_op jit(solution)/shard_map/bef,jf->bej/dot_general | solution.py:77
  31.2 0.6 %gather_fusion = f32[8,8,768]{2,1,0:T(8,128)S(1)} fusion(f32[8,8,768]{2,1,0:T(8,128)S(1)} %fusion, s32[1024]{0:T(1024)S(1)} %pad_clamp_fusion), kind=kCustom, calls=%fused_computation | custom fusion | bytes 393248 | tf_op jit(solution)/shard_map/jit(_take)/gather | solution.py:81
  32.0 1.0 %collective-permute-start.8 = (f32[16,768]{1,0:T(8,128)S(1)}, f32[16,768]{1,0:T(8,128)}, u32[]{:S(2)}, u32[]{:S(2)}) collective-permute-start(f32[16,768]{1,0:T(8,128)S(1)} %get-tuple-element.9), channel_id=1, source_target_pairs={{0,2},{1,3},{2,0},{3,1},{4,6},{5,7},{6,4},{7,5},{8,10},{9,11},{10,... | collective-permute-start | bytes 147464 | tf_op jit(solution)/shard_map/ppermute | solution.py:99
  32.9 0.9 %collective-permute-start.7 = (f32[16,768]{1,0:T(8,128)S(1)}, f32[16,768]{1,0:T(8,128)}, u32[]{:S(2)}, u32[]{:S(2)}) collective-permute-start(f32[16,768]{1,0:T(8,128)S(1)} %get-tuple-element.7), channel_id=1, source_target_pairs={{0,1},{1,0},{2,3},{3,2},{4,5},{5,4},{6,7},{7,6},{8,9},{9,8},{10,11... | collective-permute-start | bytes 147464 | tf_op jit(solution)/shard_map/ppermute | solution.py:99
  33.8 1.7 %collective-permute-done.9 = f32[16,768]{1,0:T(8,128)S(1)} collective-permute-done((f32[16,768]{1,0:T(8,128)S(1)}, f32[16,768]{1,0:T(8,128)S(1)}, u32[]{:S(2)}, u32[]{:S(2)}) %collective-permute-start.9) | collective-permute-done | bytes 49184 | tf_op jit(solution)/shard_map/ppermute | solution.py:99
  35.5 1.2 %collective-permute-done.8 = f32[16,768]{1,0:T(8,128)} collective-permute-done((f32[16,768]{1,0:T(8,128)S(1)}, f32[16,768]{1,0:T(8,128)}, u32[]{:S(2)}, u32[]{:S(2)}) %collective-permute-start.8) | collective-permute-done | bytes 49184 | tf_op jit(solution)/shard_map/ppermute | solution.py:99
  36.7 1.5 %fusion.15 = f32[16,768]{1,0:T(8,128)} fusion(f32[16,768]{1,0:T(8,128)S(1)} %collective-permute-done.9, f32[16,768]{1,0:T(8,128)} %collective-permute-done.8, f32[16,768]{1,0:T(8,128)} %collective-permute-done.7, f32[4,16,768]{2,1,0:T(8,128)S(1)} %bitcast_select_fusion, s32[]{:T(128)S(6)} %select_n.99, s32[768]{0:T(1024)S(1)} %copy-done.1, s32[16]{0:T(128)S(1)} %copy-done.2), kind=kLoop, calls=%fused_computation.23 | loop fusion | flops 61440 | bytes 248900 | tf_op jit(solution)/shard_map/jit(_where)/select_n | solution.py:103
  (24 shorter events, 0.4 us)
Async XLA Ops:
  0.0 29.2 %copy-start = (bf16[768,1,2048]{2,0,1:T(8,128)(2,1)S(1)}, bf16[768,1,2048]{2,0,1:T(8,128)(2,1)}, u32[]{:S(2)}) copy-start(bf16[768,1,2048]{2,0,1:T(8,128)(2,1)} %param.11) | copy-start | bytes 9437188
  10.2 26.5 %copy-start.1 = (s32[768]{0:T(1024)S(1)}, s32[768]{0:T(1024)}, u32[]{:S(2)}) copy-start(s32[768]{0:T(1024)} %param.12) | copy-start | bytes 9220
  10.2 26.5 %copy-start.2 = (s32[16]{0:T(128)S(1)}, s32[16]{0:T(128)}, u32[]{:S(2)}) copy-start(s32[16]{0:T(128)} %param.10) | copy-start | bytes 196
  10.8 10.0 %collective-permute-start = (bf16[8,2048]{1,0:T(8,128)(2,1)S(1)}, bf16[8,2048]{1,0:T(8,128)(2,1)S(1)}, u32[]{:S(2)}, u32[]{:S(2)}) collective-permute-start(bf16[8,2048]{1,0:T(8,128)(2,1)S(1)} %get-tuple-element.11), channel_id=1, source_target_pairs={{0,4},{2,6},{4,8},{6,10},{8,12},{10,14},{12,0},{14,2},{1,5},{3,7},... | collective-permute-start | bytes 98312 | tf_op jit(solution)/shard_map/ppermute | solution.py:74
  13.9 8.8 %collective-permute-start.1 = (bf16[8,2048]{1,0:T(8,128)(2,1)S(1)}, bf16[8,2048]{1,0:T(8,128)(2,1)S(1)}, u32[]{:S(2)}, u32[]{:S(2)}) collective-permute-start(bf16[8,2048]{1,0:T(8,128)(2,1)S(1)} %get-tuple-element.11), channel_id=1, source_target_pairs={{0,8},{2,10},{4,12},{6,14},{8,0},{10,2},{12,4},{14,6},{1,9},{3,11}... | collective-permute-start | bytes 98312 | tf_op jit(solution)/shard_map/ppermute | solution.py:74
  16.5 9.7 %collective-permute-start.2 = (bf16[8,2048]{1,0:T(8,128)(2,1)S(1)}, bf16[8,2048]{1,0:T(8,128)(2,1)S(1)}, u32[]{:S(2)}, u32[]{:S(2)}) collective-permute-start(bf16[8,2048]{1,0:T(8,128)(2,1)S(1)} %get-tuple-element.11), channel_id=1, source_target_pairs={{0,12},{2,14},{4,0},{6,2},{8,4},{10,6},{12,8},{14,10},{1,13},{3,15... | collective-permute-start | bytes 98312 | tf_op jit(solution)/shard_map/ppermute | solution.py:74
  17.8 8.9 %collective-permute-start.3 = (bf16[8,2048]{1,0:T(8,128)(2,1)S(1)}, bf16[8,2048]{1,0:T(8,128)(2,1)S(1)}, u32[]{:S(2)}, u32[]{:S(2)}) collective-permute-start(bf16[8,2048]{1,0:T(8,128)(2,1)S(1)} %get-tuple-element.10), channel_id=1, source_target_pairs={{0,2},{2,0},{4,6},{6,4},{8,10},{10,8},{12,14},{14,12},{1,3},{3,1},... | collective-permute-start | bytes 98312 | tf_op jit(solution)/shard_map/ppermute | solution.py:74
  19.3 8.0 %collective-permute-start.4 = (bf16[8,2048]{1,0:T(8,128)(2,1)S(1)}, bf16[8,2048]{1,0:T(8,128)(2,1)S(1)}, u32[]{:S(2)}, u32[]{:S(2)}) collective-permute-start(bf16[8,2048]{1,0:T(8,128)(2,1)S(1)} %get-tuple-element.10), channel_id=1, source_target_pairs={{0,6},{2,4},{4,10},{6,8},{8,14},{10,12},{12,2},{14,0},{1,7},{3,5},... | collective-permute-start | bytes 98312 | tf_op jit(solution)/shard_map/ppermute | solution.py:74
  20.8 7.1 %collective-permute-start.5 = (bf16[8,2048]{1,0:T(8,128)(2,1)S(1)}, bf16[8,2048]{1,0:T(8,128)(2,1)S(1)}, u32[]{:S(2)}, u32[]{:S(2)}) collective-permute-start(bf16[8,2048]{1,0:T(8,128)(2,1)S(1)} %get-tuple-element.10), channel_id=1, source_target_pairs={{0,10},{2,8},{4,14},{6,12},{8,2},{10,0},{12,6},{14,4},{1,11},{3,9}... | collective-permute-start | bytes 98312 | tf_op jit(solution)/shard_map/ppermute | solution.py:74
  22.7 5.9 %collective-permute-start.6 = (bf16[8,2048]{1,0:T(8,128)(2,1)S(1)}, bf16[8,2048]{1,0:T(8,128)(2,1)S(1)}, u32[]{:S(2)}, u32[]{:S(2)}) collective-permute-start(bf16[8,2048]{1,0:T(8,128)(2,1)S(1)} %get-tuple-element.10), channel_id=1, source_target_pairs={{0,14},{2,12},{4,2},{6,0},{8,6},{10,4},{12,10},{14,8},{1,15},{3,13... | collective-permute-start | bytes 98312 | tf_op jit(solution)/shard_map/ppermute | solution.py:74
  31.9 3.6 %collective-permute-start.9 = (f32[16,768]{1,0:T(8,128)S(1)}, f32[16,768]{1,0:T(8,128)S(1)}, u32[]{:S(2)}, u32[]{:S(2)}) collective-permute-start(f32[16,768]{1,0:T(8,128)S(1)} %get-tuple-element.8), channel_id=1, source_target_pairs={{0,3},{1,2},{2,1},{3,0},{4,7},{5,6},{6,5},{7,4},{8,11},{9,10},{10,... | collective-permute-start | bytes 147464 | tf_op jit(solution)/shard_map/ppermute | solution.py:99
  32.0 4.7 %collective-permute-start.8 = (f32[16,768]{1,0:T(8,128)S(1)}, f32[16,768]{1,0:T(8,128)}, u32[]{:S(2)}, u32[]{:S(2)}) collective-permute-start(f32[16,768]{1,0:T(8,128)S(1)} %get-tuple-element.9), channel_id=1, source_target_pairs={{0,2},{1,3},{2,0},{3,1},{4,6},{5,7},{6,4},{7,5},{8,10},{9,11},{10,... | collective-permute-start | bytes 147464 | tf_op jit(solution)/shard_map/ppermute | solution.py:99
  32.9 3.8 %collective-permute-start.7 = (f32[16,768]{1,0:T(8,128)S(1)}, f32[16,768]{1,0:T(8,128)}, u32[]{:S(2)}, u32[]{:S(2)}) collective-permute-start(f32[16,768]{1,0:T(8,128)S(1)} %get-tuple-element.7), channel_id=1, source_target_pairs={{0,1},{1,0},{2,3},{3,2},{4,5},{5,4},{6,7},{7,6},{8,9},{9,8},{10,11... | collective-permute-start | bytes 147464 | tf_op jit(solution)/shard_map/ppermute | solution.py:99

commit v2 on v0

v2 whole, which is shorter than its diff:
```python
import jax
import jax.numpy as jnp
from jax import lax
from jax.experimental import pallas as pl
from jax.experimental.pallas import tpu as pltpu
from jax.sharding import PartitionSpec as P

LANES = 128


def split(value):
    high = value.astype(jnp.bfloat16)
    return high, (value - high.astype(jnp.float32)).astype(jnp.bfloat16)


def precondition_kernel(counts, slots, factors, output_inverse, input_inverse, rows):
    examples, modules, tokens, width = factors.shape
    features = width // 2
    share = rows.shape[2] // features
    pack = LANES // features
    groups = share // pack
    copies = rows.shape[0] // modules
    first_row = pl.multiple_of(lax.axis_index("half") * share, 8)

    place = (examples, examples * tokens)
    example = lax.broadcasted_iota(jnp.int32, place, 0)
    column = lax.broadcasted_iota(jnp.int32, place, 1)
    kept = jnp.zeros(place, jnp.bool_)
    for e in range(examples):
        kept |= (example == e) & (column >= e * tokens) & (column < e * tokens + counts[e])
    lane = lax.broadcasted_iota(jnp.int32, (examples * tokens, LANES), 1)

    for slot in range(modules):
        module = slots[slot]
        tokens_in = factors[:, pl.ds(module, 1)].reshape(examples * tokens, width)
        twice = jnp.concatenate([tokens_in, tokens_in], axis=1)

        right = input_inverse[module]
        right = jnp.concatenate([right] * pack, axis=1)
        right = jnp.concatenate([right, jnp.zeros((features, LANES), jnp.float32)], axis=0)
        right = jnp.concatenate(split(right), axis=0)
        inner = jnp.dot(twice, right, preferred_element_type=jnp.float32)

        left = output_inverse[module, pl.ds(first_row, share)]
        left = jnp.concatenate([jnp.zeros((share, features), jnp.float32), left], axis=1)
        left = jnp.concatenate(
            [
                jnp.broadcast_to(left[pack * q + p : pack * q + p + 1], (examples, width))
                for p in range(pack)
                for q in range(groups)
            ],
            axis=0,
        )
        left = jnp.concatenate(split(left), axis=1)
        outer = lax.dot_general(
            left, twice, (((1,), (1,)), ((), ())), preferred_element_type=jnp.float32
        )
        outer = outer.reshape(pack * groups, examples, examples * tokens)
        outer = jnp.where(kept[None], outer, 0.0).reshape(pack * groups * examples, -1)

        total = jnp.zeros((groups * examples, LANES), jnp.float32)
        for p in range(pack):
            outer_high, outer_low = split(outer[p * groups * examples : (p + 1) * groups * examples])
            mine = (lane >= p * features) & (lane < (p + 1) * features)
            inner_high, inner_low = split(jnp.where(mine, inner, 0.0))
            for one, other in (
                (outer_high, inner_high),
                (outer_high, inner_low),
                (outer_low, inner_high),
            ):
                total += jnp.dot(one, other, preferred_element_type=jnp.float32)
        total = total.astype(jnp.bfloat16)
        for q in range(groups):
            block = total[q * examples : (q + 1) * examples]
            for copy in range(copies):
                rows[copy * modules + slot, :, q * LANES : (q + 1) * LANES] = block


def body(
    new_factors,
    new_counts,
    new_ids,
    replay_grads,
    replay_ids,
    slot_module,
    output_inverse,
    input_inverse,
):
    examples, module_count = new_factors.shape[:2]
    replay_count = lax.axis_size("replay")
    holders = module_count * lax.axis_size("half")
    smem = pl.BlockSpec(memory_space=pltpu.SMEM)
    vmem = pl.BlockSpec(memory_space=pltpu.VMEM)
    outgoing = pl.pallas_call(
        precondition_kernel,
        out_shape=jax.ShapeDtypeStruct(
            (replay_count * module_count, examples, replay_grads.shape[2]), jnp.bfloat16
        ),
        in_specs=[smem, smem, vmem, vmem, vmem],
        out_specs=vmem,
        compiler_params=pltpu.CompilerParams(vmem_limit_bytes=16 * 2**20),
    )(new_counts, slot_module, new_factors, output_inverse, input_inverse)
    gathered = lax.all_to_all(outgoing, ("replay", "module"), 0, 0, tiled=True)
    gathered = gathered.reshape(-1, gathered.shape[-1])
    replay_rows = replay_grads.reshape(replay_grads.shape[0], -1)
    partials = lax.dot_general(
        gathered, replay_rows, (((1,), (1,)), ((), ())), preferred_element_type=jnp.float32
    )
    partials = partials.astype(jnp.bfloat16).reshape(holders, -1, partials.shape[-1])
    terms = lax.all_to_all(partials, ("module", "half"), 0, 0, tiled=True)
    summed_scores = jnp.sum(terms.astype(jnp.float32), axis=0)
    self_pairs = new_ids[:, None] == replay_ids[None, :]
    return jnp.where(self_pairs, jnp.zeros((), jnp.float32), summed_scores)


def solution(mesh):
    in_specs = (
        P(("groups", "replay", "module"), None, None, None),
        P(("groups", "replay", "module")),
        P(("groups", "module", "half")),
        P(("groups", "replay"), "module", "half"),
        P(("groups", "replay")),
        P(),
        P(),
        P(),
    )
    out_specs = P(("groups", "module", "half"), "replay")
    return jax.shard_map(body, mesh=mesh, in_specs=in_specs, out_specs=out_specs, check_vma=False)
```

time: 70.1 us -> 30.6 us (0.44)
  waiting for transfers between devices: 20.1 us -> 0 us
  between operations: 13.5 us -> 0.03 us
  matrix products: 9.08 us -> 1.07 us
  other arithmetic: 3.53 us -> 0.71 us
  local copies, waits for them, and re-layouts: 1.37 us -> 4.1 us
  Pallas kernels: 0 us -> 1.71 us
    reduce_scatter x1 -> x0, waiting for transfers between devices: 20 us -> none  [body(): lax.psum_scatter(partials, ('module', 'half'), scatter_dimension=0, tiled...]
    all_to_all x1 -> x2, blocking collectives: 8.13 us -> 22.8 us  [the longest x1 16 us: body(): gathered = lax.all_to_all(outgoing, ('replay', 'module'), 0, 0, tiled=True)]
    all_gather x1 -> x0, blocking collectives: 14.1 us -> none  [body(): lax.all_gather(new_block, 'replay', axis=0, tiled=True)]
    dot_general x7 -> x1, matrix products: 9.08 us -> 1.07 us  [body(): lax.dot_general(gathered, replay_rows, (((1,), (1,)), ((), ())), preferre...]
    unnamed x6 -> x16, local copies, waits for them, and re-layouts: 0.01 us -> 4.1 us
    pallas_call x0 -> x1, Pallas kernels: none -> 1.71 us  [body(): pl.pallas_call(precondition_kernel, out_shape=jax.ShapeDtypeStruct((repla...]
    slice x1 -> x0, local copies, waits for them, and re-layouts: 1.18 us -> none  [body(): output_grads = slot_factors[:, :, :, feature_count:]]
    select_n x1 -> x0, other arithmetic: 1.16 us -> none  [body(): jnp.where(token_live[:, None, :, None], new_factors, jnp.zeros((), jnp.bf...]
  transfers between devices with their start and end apart: 1 -> 0, of which waited for: 1 -> 0; matrix products, arithmetic and copies ran while one was open for 0% -> 0% of each run, Pallas kernels for 0% -> 0%
where the time goes in v2:
time: 30.6 us; the launch traced here: 30.4 us
  blocking collectives  22.8 us (75%)
  local copies, waits for them, and re-layouts  4.1 us (13%)
  Pallas kernels  1.71 us (6%)
  matrix products  1.07 us (3%)
  other arithmetic  0.71 us (2%)
    all_to_all x1, blocking collectives, body(): gathered = lax.all_to_all(outgoing, ('replay', 'module'), 0, 0, tiled=True)  16 us
    all_to_all x1, blocking collectives, body(): terms = lax.all_to_all(partials, ('module', 'half'), 0, 0, tiled=True)  6.78 us
    unnamed x16, local copies, waits for them, and re-layouts  4.1 us
    pallas_call x1, Pallas kernels, body(): pl.pallas_call(precondition_kernel, out_shape=jax.ShapeDtypeStruct((repla...  1.71 us
    dot_general x1, matrix products, body(): lax.dot_general(gathered, replay_rows, (((1,), (1,)), ((), ())), preferre...  1.07 us
    select_n x1, other arithmetic, body(): return jnp.where(self_pairs, jnp.zeros((), jnp.float32), summed_scores)  0.69 us

profile of v2, /device:TPU:0, one launch (start us, length us, event | category | flops | bytes accessed | tf_op | source)
XLA Modules:
  0.0 30.4 jit_solution(166201361490040025)
XLA Ops:
  0.0 0.0 copy-start
  0.0 0.0 copy-start.1
  0.0 1.1 %copy-done.1 = bf16[8,2,64,128]{3,2,1,0:T(8,128)(2,1)S(1)} copy-done((bf16[8,2,64,128]{3,2,1,0:T(8,128)(2,1)S(1)}, bf16[8,2,64,128]{3,2,1,0:T(8,128)(2,1)}, u32[]{:S(2)}) %copy-start.1) | copy-done | bytes 262168
  1.1 0.0 copy-start.2
  1.1 0.8 %copy-done.2 = f32[2,64,64]{2,1,0:T(8,128)S(1)} copy-done((f32[2,64,64]{2,1,0:T(8,128)S(1)}, f32[2,64,64]{2,1,0:T(8,128)}, u32[]{:S(2)}) %copy-start.2) | copy-done | bytes 32792
  1.9 0.0 copy-start.3
  1.9 0.8 %copy-done.3 = f32[2,64,64]{2,1,0:T(8,128)S(1)} copy-done((f32[2,64,64]{2,1,0:T(8,128)S(1)}, f32[2,64,64]{2,1,0:T(8,128)}, u32[]{:S(2)}) %copy-start.3) | copy-done | bytes 32792
  2.8 0.0 copy-start.4
  2.8 0.7 %copy-done.4 = s32[8]{0:T(128)S(1)} copy-done((s32[8]{0:T(128)S(1)}, s32[8]{0:T(128)}, u32[]{:S(2)}) %copy-start.4) | copy-done | bytes 56
  3.4 0.0 copy-start.5
  3.4 0.7 %copy-done.5 = s32[2]{0:T(128)S(1)} copy-done((s32[2]{0:T(128)S(1)}, s32[2]{0:T(128)}, u32[]{:S(2)}) %copy-start.5) | copy-done | bytes 32
  4.1 0.0 copy-start.6
  4.1 0.0 copy-start.7
  4.1 1.7 %shard_map.82 = bf16[8,8,2048]{2,1,0:T(8,128)(2,1)S(1)} custom-call(s32[8]{0:T(128)S(1)} %copy-done.4, s32[2]{0:T(128)S(1)} %copy-done.5, bf16[8,2,64,128]{3,2,1,0:T(8,128)(2,1)S(1)} %copy-done.1, f32[2,64,64]{2,1,0:T(8,128)S(1)} %copy-done.2, f32[2,64,64]{2,1,0:T(8,128)S(1)} %copy-done.3), custom_call_target="tpu_custom_call" | custom-call | tf_op jit(solution)/shard_map/pallas_call | solution.py:94
  5.8 16.0 %all_to_all.10 = bf16[8,8,2048]{2,1,0:T(8,128)(2,1)S(1)} all-to-all(bf16[8,8,2048]{2,1,0:T(8,128)(2,1)S(1)} %shard_map.82), channel_id=1, replica_groups=mesh['groups'=2,'replay'=4,'module'=2,'half'=2] {'replay','module'}, dimensions={0} | all-to-all | bytes 524288 | tf_op jit(solution)/shard_map/all_to_all | solution.py:103
  21.8 0.0 copy-done
  21.8 1.1 %fusion.2 = bf16[64,768]{1,0:T(8,128)(2,1)S(1)} fusion(bf16[768,1,2048]{2,0,1:T(8,128)(2,1)S(1)} %copy-done, bf16[8,8,2048]{2,1,0:T(8,128)(2,1)S(1)} %all_to_all.10), kind=kOutput, calls=%fused_computation.2 | convolution fusion | flops 201375744 | bytes 3506176 | tf_op jit(solution)/shard_map/dot_general | solution.py:106
  22.9 6.8 %all_to_all.11 = bf16[4,16,768]{2,1,0:T(8,128)(2,1)S(1)} all-to-all(bf16[4,16,768]{2,1,0:T(8,128)(2,1)S(1)} %bitcast.9), channel_id=1, replica_groups=mesh['groups'=2,'replay'=4,'module'=2,'half'=2] {'module','half'}, dimensions={0} | all-to-all | bytes 196608 | tf_op jit(solution)/shard_map/all_to_all | solution.py:110
  29.7 0.0 copy-done.6
  29.7 0.0 copy-done.7
  29.7 0.7 %compare_select_fusion = f32[16,768]{1,0:T(8,128)} fusion(f32[16,768]{1,0:T(8,128)S(1)} %convert_reduce_fusion, s32[768]{0:T(1024)S(1)} %copy-done.6, s32[16]{0:T(128)S(1)} %copy-done.7), kind=kLoop, calls=%fused_computation.5 | loop fusion | flops 24576 | bytes 101440 | tf_op jit(solution)/shard_map/jit(_where)/select_n | solution.py:113
  (1 shorter events, 0.0 us)
Async XLA Ops:
  0.0 21.8 %copy-start = (bf16[768,1,2048]{2,0,1:T(8,128)(2,1)S(1)}, bf16[768,1,2048]{2,0,1:T(8,128)(2,1)}, u32[]{:S(2)}) copy-start(bf16[768,1,2048]{2,0,1:T(8,128)(2,1)} %param.11) | copy-start | bytes 9437188
  0.0 1.1 %copy-start.1 = (bf16[8,2,64,128]{3,2,1,0:T(8,128)(2,1)S(1)}, bf16[8,2,64,128]{3,2,1,0:T(8,128)(2,1)}, u32[]{:S(2)}) copy-start(bf16[8,2,64,128]{3,2,1,0:T(8,128)(2,1)} %factors.1) | copy-start | bytes 786436
  1.1 0.8 %copy-start.2 = (f32[2,64,64]{2,1,0:T(8,128)S(1)}, f32[2,64,64]{2,1,0:T(8,128)}, u32[]{:S(2)}) copy-start(f32[2,64,64]{2,1,0:T(8,128)} %output_inverse.1) | copy-start | bytes 98308
  1.9 0.8 %copy-start.3 = (f32[2,64,64]{2,1,0:T(8,128)S(1)}, f32[2,64,64]{2,1,0:T(8,128)}, u32[]{:S(2)}) copy-start(f32[2,64,64]{2,1,0:T(8,128)} %input_inverse.1) | copy-start | bytes 98308
  2.8 0.7 %copy-start.4 = (s32[8]{0:T(128)S(1)}, s32[8]{0:T(128)}, u32[]{:S(2)}) copy-start(s32[8]{0:T(128)} %counts.1) | copy-start | bytes 100
  3.4 0.7 %copy-start.5 = (s32[2]{0:T(128)S(1)}, s32[2]{0:T(128)}, u32[]{:S(2)}) copy-start(s32[2]{0:T(128)} %slots.1) | copy-start | bytes 28
  4.1 25.6 %copy-start.6 = (s32[768]{0:T(1024)S(1)}, s32[768]{0:T(1024)}, u32[]{:S(2)}) copy-start(s32[768]{0:T(1024)} %param.12) | copy-start | bytes 9220
  4.1 25.6 %copy-start.7 = (s32[16]{0:T(128)S(1)}, s32[16]{0:T(128)}, u32[]{:S(2)}) copy-start(s32[16]{0:T(128)} %param.10) | copy-start | bytes 196
